TPU v7x, 1024 devices: a whole 8x8x8 slice. The times are simulated.
1024 devices in a mesh: img: 64 (over y, z_hi, core), txt: 16 (over x, z_lo).
Axes of the slice: x: 8, y: 8, z: 8 (z_hi: 4, z_lo: 2; z = z_hi * 2 + z_lo), core: 2. Of those that a mesh axis runs over, the one named last changes fastest.
Arguments:
- images: bfloat16 [16384, 1152], P(('img', 'txt')), may hold values from -6 to 6
- texts: bfloat16 [16384, 1152], P(('txt', 'img')), may hold values from -6 to 6
- log_temp: float32 [1], replicated, may hold values from 1.6 to 2.3
- bias: float32 [1], replicated, may hold values from -7 to -5
Outputs:
- loss: float32 [1], replicated
- grad_images: float32 [16384, 1152], P(('img', 'txt'))
- grad_texts: float32 [16384, 1152], P(('txt', 'img'))
- grad_temp: float32 [1], replicated
- grad_bias: float32 [1], replicated
All inputs are finite; a program needn't handle non-finite values.
Results may differ from a plain program's by a relative error of at most 0.0043.
Values may be sent and summed in bfloat16 or wider, within the bound.
A program may use at most 32 MiB of HBM per device.

v0:
```python
import jax
import jax.numpy as jnp
from jax import lax
from jax.sharding import PartitionSpec as P


def normalize(embed):
    wide = embed.astype(jnp.float32)
    inverse = lax.rsqrt(jnp.sum(wide * wide, axis=-1, keepdims=True) + 1e-06)
    return (wide * inverse, inverse)


def unnormalize(normed, inverse, grad_normed):
    inner = jnp.sum(normed * grad_normed, axis=-1, keepdims=True)
    return inverse * (grad_normed - normed * inner)


def body(images, texts, log_temp, bias):
    x_norm, inv_x = normalize(images)
    y_norm, inv_y = normalize(texts)
    x_block = lax.all_gather(x_norm.astype(jnp.bfloat16), "txt", axis=0, tiled=True)
    y_block = lax.all_gather(y_norm.astype(jnp.bfloat16), "img", axis=0, tiled=True)
    img_count = x_block.shape[0]
    txt_count = y_block.shape[0]
    row_first = lax.axis_index("img") * img_count
    col_first = lax.axis_index("txt") * txt_count
    temp = jnp.exp(log_temp[0])
    shift = bias[0]
    dots = jnp.dot(x_block, y_block.T, preferred_element_type=jnp.float32)
    logits = temp * dots + shift
    row_ids = row_first + jnp.arange(img_count, dtype=jnp.int32)
    col_ids = col_first + jnp.arange(txt_count, dtype=jnp.int32)
    sign = jnp.where(row_ids[:, None] == col_ids[None, :], 1.0, -1.0).astype(jnp.float32)
    loss_part = -jnp.sum(jax.nn.log_sigmoid(sign * logits))
    grad_logits = -sign * jax.nn.sigmoid(-sign * logits)
    temp_part = jnp.sum(grad_logits * dots)
    bias_part = jnp.sum(grad_logits)
    grad_low = grad_logits.astype(jnp.bfloat16)
    dx_part = temp * jnp.dot(grad_low, y_block, preferred_element_type=jnp.float32)
    dy_norm = lax.psum_scatter(
        temp * jnp.dot(grad_low.T, x_block, preferred_element_type=jnp.float32),
        "img",
        scatter_dimension=0,
        tiled=True,
    )
    partials = jnp.stack([loss_part, temp_part, bias_part])
    dx_norm = lax.psum_scatter(dx_part, "txt", scatter_dimension=0, tiled=True)
    totals = lax.psum(partials, ("img", "txt"))
    batch_total = img_count * lax.axis_size("img")
    grad_images = unnormalize(x_norm, inv_x, dx_norm)
    grad_texts = unnormalize(y_norm, inv_y, dy_norm)
    loss = (totals[0] / batch_total).reshape(1)
    grad_temp = (temp * totals[1] / batch_total).reshape(1)
    grad_bias = (totals[2] / batch_total).reshape(1)
    return (loss, grad_images, grad_texts, grad_temp, grad_bias)


def solution(mesh):
    in_specs = (P(("img", "txt"), None), P(("txt", "img"), None), P(), P())
    out_specs = (P(), P(("img", "txt"), None), P(("txt", "img"), None), P(), P())
    return jax.shard_map(body, mesh=mesh, in_specs=in_specs, out_specs=out_specs, check_vma=False)
```

profile of v0, /device:TPU:1, one launch (start us, length us, event | category | flops | bytes accessed | tf_op | source)
XLA Modules:
  0.0 380.9 jit_solution(12328581597111419198)
XLA Ops:
  7.2 0.0 all-gather.2.cloned.1.call-start
  7.2 0.9 fusion.23
  8.1 1.5 fusion.12
  9.6 0.0 all-gather.2.cloned.1.call-update
  9.6 0.0 reduce-scatter.3.cloned.1.call-start
  11.0 0.9 fusion.19
  11.9 0.9 fusion.15
  12.8 32.2 %all_gather.6 = bf16[256,1152]{1,0:T(8,128)(2,1)S(1)} all-gather(bf16[16,1152]{1,0:T(8,128)(2,1)S(1)} %fusion.15), channel_id=1, replica_groups=mesh['img'=64,'txt'=16] {'txt'}, dimensions={0}, use_global_device_ids=true | all-gather | bytes 626688 | tf_op jit(solution)/shard_map/all_gather | solution.py:21
  45.0 73.6 %all-gather.2.cloned.1.call-done = bf16[1024,1152]{1,0:T(8,128)(2,1)} async-done(((bf16[16,1152]{1,0:T(8,128)(2,1)}), bf16[1024,1152]{1,0:T(8,128)(2,1)}) %all-gather.2.cloned.1.call-update) | async-done | bytes 2359312 | tf_op jit(solution)/shard_map/all_gather | solution.py:22
  118.6 0.0 copy-start.2
  118.6 4.3 %fusion.7 = (f32[]{:T(128)}, f32[]{:T(128)}, f32[]{:T(128)}, f32[256,1024]{1,0:T(8,128)S(1)}) fusion(f32[]{:T(128)} %bitcast.11, f32[]{:T(128)} %bitcast, s32[1024]{0:T(1024)S(1)} %iota_add_fusion, s32[256]{0:T(256)S(1)} %iota_add_fusion.1, bf16[256,1152]{1,0:T(8,128)(2,1)S(1)} %all_gather.6, bf16[1024,1152]{1,0:T(8,128)(2,1)} %all-gather.2.cloned.1.call-done), kind=kOutput, calls=%fused_computation.12 | convolution fusion | flops 609746944 | bytes 4002836 | tf_op jit(solution)/shard_map/dot_general | solution.py:29
  122.9 0.0 copy-done.2
  122.9 2.1 convolution_multiply_fusion.1
  125.0 0.0 reduce-scatter.3.cloned.1.call-update
  125.0 0.0 reduce-scatter.5.cloned.1.call-start
  125.1 3.3 convolution_multiply_fusion
  128.4 0.0 copy-start
  128.4 0.0 copy-start.1
  128.5 0.0 reduce-scatter.5.cloned.1.call-update
  128.5 2.0 pad_maximum_fusion
  130.5 112.1 %psum.7 = f32[3]{0:T(128)S(1)} all-reduce(f32[3]{0:T(128)S(1)} %pad_maximum_fusion), channel_id=1, replica_groups=mesh['img'=64,'txt'=16] {'img','txt'}, use_global_device_ids=true, to_apply=%region_5.6 | all-reduce | flops 3 | bytes 24 | tf_op jit(solution)/shard_map/psum | solution.py:48
  242.6 0.6 fusion.27
  245.2 0.0 reduce-scatter.3.cloned.1.call-done
  245.2 0.0 copy-done
  245.2 1.1 fusion.16
  246.3 1.6 fusion.18
  247.9 120.4 %reduce-scatter.5.cloned.1.call-done = f32[16,1152]{1,0:T(8,128)} async-done(((f32[1024,1152]{1,0:T(8,128)}), f32[16,1152]{1,0:T(8,128)}) %reduce-scatter.5.cloned.1.call-update) | async-done | bytes 73744 | tf_op jit(solution)/shard_map/reduce_scatter | solution.py:40
  368.3 0.0 copy-done.1
  368.3 1.1 fusion.20
  369.4 1.6 fusion.22
  (4 shorter events, 0.0 us)
Async XLA Ops:
  7.2 111.5 %all-gather.2.cloned.1.call-start = ((), (), s32[]{:S(2)}) async-start(), calls=%async_computation.2 | async-start | bytes 2396160 | tf_op jit(solution)/shard_map/all_gather | solution.py:22
  9.6 235.6 %reduce-scatter.3.cloned.1.call-start = ((), (), s32[]{:S(2)}) async-start(), calls=%async_computation.3 | async-start | bytes 1253376 | tf_op jit(solution)/shard_map/reduce_scatter | solution.py:47
  118.6 4.3 %copy-start.2 = (bf16[1024,1152]{1,0:T(8,128)(2,1)S(1)}, bf16[1024,1152]{1,0:T(8,128)(2,1)}, u32[]{:S(2)}) copy-start(bf16[1024,1152]{1,0:T(8,128)(2,1)} %all-gather.2.cloned.1.call-done) | copy-start | bytes 7077892
  125.0 243.3 %reduce-scatter.5.cloned.1.call-start = ((), (), s32[]{:S(2)}) async-start(), calls=%async_computation.4 | async-start | bytes 4792320 | tf_op jit(solution)/shard_map/reduce_scatter | solution.py:40
  128.4 116.8 %copy-start = (bf16[16,1152]{1,0:T(8,128)(2,1)S(1)}, bf16[16,1152]{1,0:T(8,128)(2,1)}, u32[]{:S(2)}) copy-start(bf16[16,1152]{1,0:T(8,128)(2,1)} %param.4) | copy-start | bytes 110596
  128.4 239.9 %copy-start.1 = (bf16[16,1152]{1,0:T(8,128)(2,1)S(1)}, bf16[16,1152]{1,0:T(8,128)(2,1)}, u32[]{:S(2)}) copy-start(bf16[16,1152]{1,0:T(8,128)(2,1)} %param.5) | copy-start | bytes 110596
Sparse Core Ops, SparseCore 0:
  13.0 105.5 all-gather.1
  125.2 61.6 reduce-scatter.2
  192.8 175.5 reduce-scatter.4
where the time goes:
time: 385 us; the launch traced here: 381 us
  waiting for transfers between devices  194 us (50%)
  blocking collectives  144 us (37%)
  between operations  20.5 us (5%)
  other arithmetic  11.5 us (3%)
  matrix products  9.75 us (3%)
    reduce_scatter x1, waiting for transfers between devices, body(): lax.psum_scatter(temp * jnp.dot(grad_low.T, x_block, preferred_element_ty...  120 us
    psum x1, blocking collectives, body(): totals = lax.psum(partials, ('img', 'txt'))  112 us
    all_gather x1, waiting for transfers between devices, body(): lax.all_gather(y_norm.astype(jnp.bfloat16), 'img', axis=0, tiled=True)  73.6 us
    all_gather x1, blocking collectives, body(): lax.all_gather(x_norm.astype(jnp.bfloat16), 'txt', axis=0, tiled=True)  32.2 us
  transfers between devices with their start and end apart: 3, of which 2 were waited for; matrix products, arithmetic and copies ran while one was open for 3% of the time, Pallas kernels for 0%

commit v1 on v0

v1 whole, which is shorter than its diff:
```python
import functools

import jax
import jax.numpy as jnp
from jax import lax
from jax.experimental import pallas as pl
from jax.experimental.pallas import tpu as pltpu
from jax.sharding import PartitionSpec as P

MESH = pl.DeviceIdType.MESH
F32, BF16 = jnp.float32, jnp.bfloat16
NX, NY, NZ = 8, 8, 4
ROWS = 16
FAR_FIRST = (4, 3, 5, 2, 6, 1, 7)


def normalize(embed):
    wide = embed.astype(F32)
    inverse = lax.rsqrt(jnp.sum(wide * wide, axis=-1, keepdims=True) + 1e-06)
    return wide * inverse, inverse


def unnormalize(normed, inverse, grad_normed):
    inner = jnp.sum(normed * grad_normed, axis=-1, keepdims=True)
    return inverse * (grad_normed - normed * inner)


def kernel(
    log_temp_ref, bias_ref, images_ref, texts_ref,
    loss_ref, grad_images_ref, grad_texts_ref, grad_temp_ref, grad_bias_ref,
    XB, YB, GT, DYF, DYB, RY, RZ, RZ1, RY1, TOT, DYN, DXS, RXS, DX0, DXB, RX, RXZ, DXT, PA, PB, PC,
    ss, rs,
):
    img, txt = lax.axis_index("img"), lax.axis_index("txt")
    y, zh, c = img // (NZ * 2), (img // 2) % NZ, img % 2
    x, zl = txt // 2, txt % 2
    width = images_ref.shape[1]

    def device(dx=0, dy=0, dz=0, dl=0, dc=0):
        i = ((((y + dy) % NY) * NZ + (zh + dz) % NZ) * 2) + (c + dc) % 2
        t = ((x + dx) % NX) * 2 + (zl + dl) % 2
        return (i, t)

    names = {}
    sends = {"all": [], 0: [], 1: []}

    def copy_of(name):
        q, src, dst, to = names[name]
        return pltpu.make_async_remote_copy(
            src_ref=src(), dst_ref=dst(), send_sem=ss.at[q], recv_sem=rs.at[q],
            device_id=device(**to), device_id_type=MESH,
        )

    def send(name, src, dst, to, who="all"):
        q = names[name][0] if name in names else len(names)
        names[name] = (q, src, dst, to)
        copy_of(name).start()
        sends[who].append(name)

    def wait(name):
        copy_of(name).wait_recv()

    others = [device(dz=m, dl=a, dc=b) for m in range(NZ) for a in (0, 1) for b in (0, 1) if (m, a, b) != (0, 0, 0)]
    peers = [device(dx=j) for j in range(1, NX)] + [device(dy=j) for j in range(1, NY)] + others
    barrier = pltpu.get_barrier_semaphore()
    for peer in peers:
        pl.semaphore_signal(barrier, inc=1, device_id=peer, device_id_type=MESH)

    x_norm, inv_x = normalize(images_ref[...])
    y_norm, inv_y = normalize(texts_ref[...])
    XB[0, 0, 0] = x_norm.astype(BF16)
    YB[0, 0] = y_norm.astype(BF16)
    pl.semaphore_wait(barrier, len(peers))

    def text_z_own(who):
        for m in (2, 1, 3):
            send(f"tz{m}", lambda m=m: YB.at[0, 0], lambda m=m: YB.at[0, NZ - m], dict(dz=m), who)

    def text_y_own(who):
        for j in FAR_FIRST:
            send(f"ty{j}", lambda j=j: YB.at[0, 0], lambda j=j: YB.at[NY - j, 0], dict(dy=j), who)

    @pl.when(c == 0)
    def _():
        text_z_own(0)

    @pl.when(c == 1)
    def _():
        text_y_own(1)

    send("xl", lambda: XB.at[0, 0, 0], lambda: XB.at[0, 0, 1], dict(dl=1))
    for j in FAR_FIRST:
        send(f"xo{j}", lambda j=j: XB.at[0, 0, 0], lambda j=j: XB.at[0, NX - j, 0], dict(dx=j))

    @pl.when(c == 0)
    def _():
        text_y_own(0)
        for m in (1, 3, 2):
            wait(f"tz{m}")
        for j in FAR_FIRST:
            send(f"tr{j}", lambda j=j: YB.at[0, pl.ds(1, 3)], lambda j=j: YB.at[NY - j, pl.ds(1, 3)], dict(dy=j), 0)

    @pl.when(c == 1)
    def _():
        text_z_own(1)

    wait("xl")
    for j in FAR_FIRST:
        send(f"xp{j}", lambda j=j: XB.at[0, 0, 1], lambda j=j: XB.at[0, NX - j, 1], dict(dx=j))
    send("xs0", lambda: XB.at[0, 0], lambda: XB.at[1, 0], dict(dc=1))

    @pl.when(c == 1)
    def _():
        for j in (1, 7, 2, 6, 3, 5, 4):
            wait(f"ty{j}")
        for m in (2, 1, 3):
            send(f"tw{m}", lambda m=m: YB.at[pl.ds(1, 7), 0], lambda m=m: YB.at[pl.ds(1, 7), NZ - m], dict(dz=m), 1)

    for j in (1, 7, 2, 6, 3, 5, 4):
        wait(f"xo{j}")
        wait(f"xp{j}")
        send(f"xs{NX - j}", lambda j=j: XB.at[0, NX - j], lambda j=j: XB.at[1, NX - j], dict(dc=1))
    for k in range(NX):
        wait(f"xs{k}")

    @pl.when(c == 0)
    def _():
        for j in (1, 7, 2, 6, 3, 5, 4):
            wait(f"ty{j}")
            wait(f"tr{j}")

    @pl.when(c == 1)
    def _():
        for m in (1, 3, 2):
            wait(f"tz{m}")
            wait(f"tw{m}")

    temp = jnp.exp(jnp.full((1, 128), log_temp_ref[0], F32))
    temp_row = jnp.exp(jnp.full((1, 512), log_temp_ref[0], F32))
    shift = bias_ref[0]
    col = lax.broadcasted_iota(jnp.int32, (1, 512), 1)
    col_core = (c + (col >> 8)) & 1
    col_x = (x + ((col >> 5) & 7)) & 7
    col_zl = (zl + ((col >> 4) & 1)) & 1
    col_id = ((y * NZ + zh) * 2 + col_core) * 256 + (col_x * 2 + col_zl) * ROWS + (col & 15)
    row = lax.broadcasted_iota(jnp.int32, (128, 1), 0)
    parts = [jnp.zeros((1, 512), F32) for _ in range(3)]
    for first in (4, 2, 6, 0):
        row_y = (y + first + (row >> 6)) & 7
        row_zh = (zh + ((row >> 4) & 3)) & 3
        row_id = (x * 2 + zl) * 1024 + ((row_y * NZ + row_zh) * 2 + c) * ROWS + (row & 15)
        rows_y = YB[pl.ds(first, 2)].reshape(128, width)
        cols_x = XB[...].reshape(512, width)
        dots = lax.dot_general(rows_y, cols_x, (((1,), (1,)), ((), ())), preferred_element_type=F32)
        logits = temp_row * dots + shift
        match = row_id == col_id
        signed = jnp.where(match, -logits, logits)
        decay = jnp.exp(-jnp.abs(signed))
        total = 1.0 + decay
        loss = jnp.maximum(signed, 0.0) + jnp.log1p(decay)
        sig = jnp.where(signed >= 0, 1.0, decay) / total
        grad = jnp.where(match, -sig, sig)
        for n, value in enumerate((loss, grad * dots, grad)):
            parts[n] = parts[n] + jnp.sum(value, axis=0, keepdims=True)
        low = grad.astype(BF16)
        GT[pl.ds(first * 64, 128)] = low
        dy = jnp.dot(low, cols_x, preferred_element_type=F32).reshape(2, NZ, ROWS, width)
        DYF[pl.ds(first, 2)] = dy
        DYB[pl.ds(first, 2)] = dy.astype(BF16)

        @pl.when(c == 0)
        def _():
            for j in (first, first + 1):
                if j:
                    send(f"dy{j}", lambda j=j: DYB.at[j], lambda j=j: RY.at[j - 1], dict(dy=j), 0)

    @pl.when(c == 1)
    def _():
        for m in (2, 1, 3):
            send(f"dz{m}", lambda m=m: DYB.at[:, m], lambda m=m: RZ1.at[m - 1], dict(dz=m), 1)

    folded = [part[:, 0:128] + part[:, 128:256] + part[:, 256:384] + part[:, 384:512] for part in parts]
    PA[0] = jnp.concatenate(folded + [jnp.zeros((5, 128), F32)], axis=0)
    for j in FAR_FIRST:
        send(f"pa{j}", lambda j=j: PA.at[0], lambda j=j: PA.at[NX - j], dict(dx=j))

    texts_all = YB[...].reshape(512, width)
    over_texts = (((0,), (0,)), ((), ()))
    DXS[...] = lax.dot_general(GT[:, 256:512], texts_all, over_texts, preferred_element_type=F32).reshape(NX, 2, ROWS, width)
    for k in (4, 2, 6, 0):
        send(f"sx{k}", lambda k=k: DXS.at[pl.ds(k, 2)], lambda k=k: RXS.at[pl.ds(k, 2)], dict(dc=1))
    DX0[...] = lax.dot_general(GT[:, 0:256], texts_all, over_texts, preferred_element_type=F32).reshape(NX, 2, ROWS, width)
    for k in (4, 2, 6, 0):
        wait(f"sx{k}")
        both = DX0[pl.ds(k, 2)] + RXS[pl.ds(k, 2)]
        DXB[pl.ds(k, 2)] = both.astype(BF16)
        if k == 0:
            DXT[...] = both[0]
        for j in (k, k + 1):
            if j:
                send(f"dx{j}", lambda j=j: DXB.at[j], lambda j=j: RX.at[j - 1], dict(dx=j))

    for j in (1, 7, 2, 6, 3, 5, 4):
        wait(f"pa{j}")
    total = PA[(0 - x) % NX]
    for a in range(1, NX):
        total = total + PA[(a - x) % NX]
    PB[0] = total
    for j in FAR_FIRST:
        send(f"pb{j}", lambda j=j: PB.at[0], lambda j=j: PB.at[NY - j], dict(dy=j))

    @pl.when(c == 0)
    def _():
        for j in (1, 7, 2, 6, 3, 5, 4):
            wait(f"dy{j}")
        for m in (2, 1, 3, 0):
            part = DYF[0, m]
            for j in range(1, NY):
                part = part + RY[j - 1, m].astype(F32)
            TOT[m] = part
            if m:
                send(f"ez{m}", lambda m=m: TOT.at[m], lambda m=m: RZ.at[m - 1], dict(dz=m), 0)

    @pl.when(c == 1)
    def _():
        for m in (1, 3, 2):
            wait(f"dz{m}")
        for j in FAR_FIRST + (0,):
            part = DYF[j, 0]
            for m in range(1, NZ):
                part = part + RZ1[m - 1, j].astype(F32)
            TOT[j] = part
            if j:
                send(f"ey{j}", lambda j=j: TOT.at[j], lambda j=j: RY1.at[j - 1], dict(dy=j), 1)

    for j in (1, 7, 2, 6, 3, 5, 4):
        wait(f"pb{j}")
    total = PB[(0 - y) % NY]
    for a in range(1, NY):
        total = total + PB[(a - y) % NY]
    PC[0] = total
    for m in range(NZ):
        for a in (0, 1):
            for b in (0, 1):
                if (m, a, b) != (0, 0, 0):
                    send(f"pc{m}{a}{b}", lambda m=m, a=a, b=b: PC.at[0], lambda m=m, a=a, b=b: PC.at[((NZ - m) % NZ) * 4 + a * 2 + b], dict(dz=m, dl=a, dc=b))

    for j in (1, 7, 2, 6, 3, 5, 4):
        wait(f"dx{j}")
    part = DXT[1]
    for j in range(1, NX):
        part = part + RX[j - 1, 1].astype(F32)
    DXT[1] = part
    send("ex", lambda: DXT.at[1], lambda: RXZ, dict(dl=1))
    part = DXT[0]
    for j in range(1, NX):
        part = part + RX[j - 1, 0].astype(F32)
    DXT[0] = part

    for m in range(NZ):
        for a in (0, 1):
            for b in (0, 1):
                if (m, a, b) != (0, 0, 0):
                    wait(f"pc{m}{a}{b}")
    total = None
    for m in range(NZ):
        for a in (0, 1):
            for b in (0, 1):
                term = PC[((m - zh) % NZ) * 4 + ((a - zl) % 2) * 2 + (b - c) % 2]
                total = term if total is None else total + term
    batch = float(images_ref.shape[0] * NX * NY * NZ * 4)
    loss_ref[0] = jnp.sum(total[0:1]) / batch
    grad_temp_ref[0] = jnp.sum(temp * total[1:2]) / batch
    grad_bias_ref[0] = jnp.sum(total[2:3]) / batch

    scale = jnp.exp(jnp.full((1, width), log_temp_ref[0], F32))

    @pl.when(c == 0)
    def _():
        part = TOT[0]
        for m in range(1, NZ):
            wait(f"ez{m}")
            part = part + RZ[m - 1]
        DYN[...] = part

    @pl.when(c == 1)
    def _():
        part = TOT[0]
        for j in range(1, NY):
            wait(f"ey{j}")
            part = part + RY1[j - 1]
        DYN[...] = part

    grad_texts_ref[...] = unnormalize(y_norm, inv_y, scale * DYN[...])
    wait("ex")
    grad_images_ref[...] = unnormalize(x_norm, inv_x, scale * (DXT[0] + RXZ[...]))

    for name in sends["all"]:
        copy_of(name).wait_send()
    for core in (0, 1):

        @pl.when(c == core)
        def _():
            for name in sends[core]:
                copy_of(name).wait_send()


def body(images, texts, log_temp, bias):
    rows, width = images.shape
    smem = pl.BlockSpec(memory_space=pltpu.SMEM)
    vmem = pl.BlockSpec(memory_space=pltpu.VMEM)
    scalar = jax.ShapeDtypeStruct((1,), F32)
    wide = jax.ShapeDtypeStruct((rows, width), F32)
    piece = (rows, width)
    scratch = [
        ((2, NX, 2) + piece, BF16),
        ((NY, NZ) + piece, BF16),
        ((512, 512), BF16),
        ((NY, NZ) + piece, F32),
        ((NY, NZ) + piece, BF16),
        ((NY - 1, NZ) + piece, BF16),
        ((NZ - 1,) + piece, F32),
        ((NZ - 1, NY) + piece, BF16),
        ((NY - 1,) + piece, F32),
        ((NY,) + piece, F32),
        (piece, F32),
        ((NX, 2) + piece, F32),
        ((NX, 2) + piece, F32),
        ((NX, 2) + piece, F32),
        ((NX, 2) + piece, BF16),
        ((NX - 1, 2) + piece, BF16),
        (piece, F32),
        ((2,) + piece, F32),
        ((NX, 8, 128), F32),
        ((NY, 8, 128), F32),
        ((16, 8, 128), F32),
    ]
    return pl.pallas_call(
        kernel,
        out_shape=(scalar, wide, wide, scalar, scalar),
        in_specs=[smem, smem, vmem, vmem],
        out_specs=(smem, vmem, vmem, smem, smem),
        scratch_shapes=[pltpu.VMEM(shape, kind) for shape, kind in scratch]
        + [pltpu.SemaphoreType.DMA((128,)), pltpu.SemaphoreType.DMA((128,))],
        compiler_params=pltpu.CompilerParams(collective_id=0, has_side_effects=True, vmem_limit_bytes=48 * 2**20),
        name="sigmoid_loss",
    )(log_temp, bias, images, texts)


def solution(mesh):
    in_specs = (P(("img", "txt"), None), P(("txt", "img"), None), P(), P())
    out_specs = (P(), P(("img", "txt"), None), P(("txt", "img"), None), P(), P())
    return jax.shard_map(body, mesh=mesh, in_specs=in_specs, out_specs=out_specs, check_vma=False)
```

time: 385 us -> 83.4 us (0.22)
  the two profiles are of different devices: /device:TPU:1 before, /device:TPU:29 now
where the time goes in v1:
time: 83.4 us; the launch traced here: 83.1 us
  Pallas kernels  73.1 us (88%)
  between operations  7.18 us (9%)
  local copies, waits for them, and re-layouts  2.8 us (3%)
    pallas_call x1, Pallas kernels, body(): pl.pallas_call(kernel, out_shape=(scalar, wide, wide, scalar, scalar), in...  73.1 us
    unnamed x6, local copies, waits for them, and re-layouts  2.8 us

profile of v1, /device:TPU:29, one launch (start us, length us, event | category | flops | bytes accessed | tf_op | source)
XLA Modules:
  0.0 83.1 jit_solution(5493390218697241136)
XLA Ops:
  1.9 0.0 copy-start
  1.9 0.8 copy-done
  2.7 0.0 copy-start.1
  2.7 0.8 copy-done.1
  3.5 73.1 %sigmoid_loss.1 = (f32[1]{0:T(128)}, f32[16,1152]{1,0:T(8,128)S(1)}, f32[16,1152]{1,0:T(8,128)S(1)}, f32[1]{0:T(128)}, f32[1]{0:T(128)}) custom-call(f32[1]{0:T(128)S(6)} %copy.14.log_temp_ref, f32[1]{0:T(128)S(6)} %copy.15.bias_ref, bf16[16,1152]{1,0:T(8,128)(2,1)S(1)} %copy-done, bf16[16,1152]{1,0:T(8,128)(2,1)S(1)} %copy-done.1), custom_call_target="tpu_custom_call" | custom-call | tf_op jit(solution)/shard_map/sigmoid_loss/pallas_call | solution.py:338
  77.2 0.6 copy.17
  77.8 0.6 copy.18
Async XLA Ops:
  1.9 0.8 copy-start
  2.7 0.8 copy-start.1

commit v2 on v0

v2 whole, which is shorter than its diff:
```python
import jax
import jax.numpy as jnp
from jax import lax
from jax.experimental import pallas as pl
from jax.experimental.pallas import tpu as pltpu
from jax.sharding import PartitionSpec as P

MESH = pl.DeviceIdType.MESH
F32, BF16 = jnp.float32, jnp.bfloat16
NX, NY, NZ = 8, 8, 4
ROWS = 16
VMEM_LIMIT = 48 * 2**20
FAR_FIRST = (4, 3, 5, 2, 6, 1, 7)
NEAR_FIRST = (1, 7, 2, 6, 3, 5, 4)
LAST_Z = {4: (1, 3, 2), 3: (1, 3), 5: (1, 3), 2: (1,), 6: (3,)}
LAST_Y = {1: (1, 3), 7: (1, 3), 3: (2, 1), 5: (2, 1), 2: (2, 2), 6: (1, 2)}
FAR = (3, 4, 5)
NEAR = (1, 7, 2, 6)


def normalize(embed):
    wide = embed.astype(F32)
    inverse = lax.rsqrt(jnp.sum(wide * wide, axis=-1, keepdims=True) + 1e-06)
    return wide * inverse, inverse


def unnormalize(normed, inverse, grad_normed):
    inner = jnp.sum(normed * grad_normed, axis=-1, keepdims=True)
    return inverse * (grad_normed - normed * inner)


def kernel(
    log_temp_ref, bias_ref, images_ref, texts_ref,
    grad_images_ref, grad_texts_ref, sums_ref,
    XB, YB, GT, DYF, DYB, RY, RZ1, RY1, RZ, DYO, DXS, RXS, DX0, DXB, RX, RXL, RX2, RXZ, PA, PB, PC,
    ss, rs,
):
    img, txt = lax.axis_index("img"), lax.axis_index("txt")
    y, zh, c = img // (NZ * 2), (img // 2) % NZ, img % 2
    x, zl = txt // 2, txt % 2
    width = images_ref.shape[1]

    def device(dx=0, dy=0, dz=0, dl=0, dc=0):
        i = ((((y + dy) % NY) * NZ + (zh + dz) % NZ) * 2) + (c + dc) % 2
        t = ((x + dx) % NX) * 2 + (zl + dl) % 2
        return (i, t)

    sent = {}

    def send(name, src, dst, **to):
        q = len(sent)
        sent[name] = pltpu.make_async_remote_copy(
            src_ref=src, dst_ref=dst, send_sem=ss.at[q], recv_sem=rs.at[q],
            device_id=device(**to), device_id_type=MESH,
        )
        sent[name].start()

    def wait(name):
        sent[name].wait_recv()

    others = [dict(dz=m, dl=a, dc=b) for m in range(NZ) for a in (0, 1) for b in (0, 1) if (m, a, b) != (0, 0, 0)]
    peers = [dict(dx=j) for j in range(1, NX)] + [dict(dy=j) for j in range(1, NY)] + others
    barrier = pltpu.get_barrier_semaphore()
    for peer in peers:
        pl.semaphore_signal(barrier, inc=1, device_id=device(**peer), device_id_type=MESH)

    x_norm, inv_x = normalize(images_ref[...])
    y_norm, inv_y = normalize(texts_ref[...])
    XB[0, 0, 0] = x_norm.astype(BF16)
    YB[0, 0] = y_norm.astype(BF16)
    pl.semaphore_wait(barrier, len(peers))

    for m in (1, 3, 2):
        send(f"tz{NZ - m}", YB.at[0, 0], YB.at[0, NZ - m], dz=m)
    send("xl", XB.at[0, 0, 0], XB.at[0, 0, 1], dl=1)
    for j in FAR_FIRST:
        send(f"ty{NY - j}", YB.at[0, 0], YB.at[NY - j, 0], dy=j)
        send(f"xo{NX - j}", XB.at[0, 0, 0], XB.at[0, NX - j, 0], dx=j)
    wait("xl")
    for k in (2, 6, 1, 7):
        send(f"xp{k}", XB.at[0, 0, 1], XB.at[0, k, 1], dx=NX - k)
    for r in (1, 3, 2):
        wait(f"tz{r}")
    for k in (1, 7, 3, 5):
        r, n = LAST_Y[k]
        send(f"tp{k}", YB.at[0, pl.ds(r, n)], YB.at[k, pl.ds(r, n)], dy=NY - k)
    send("xs0", XB.at[0, 0], XB.at[1, 0], dc=1)
    for k, rs_of in LAST_Z.items():
        wait(f"ty{k}")
        for r in rs_of:
            send(f"tw{k}{r}", YB.at[k, 0], YB.at[k, r], dz=NZ - r)
        if k in FAR:
            wait(f"xo{k}")
            send(f"xq{k}", XB.at[0, k, 0], XB.at[0, k, 1], dl=1)
    for k, near, to in ((2, 1, NY - 1), (6, 7, 1)):
        r, n = LAST_Y[k]
        wait(f"tp{near}")
        send(f"tp{k}", YB.at[near, pl.ds(r, n)], YB.at[k, pl.ds(r, n)], dy=to)
    for k in (1, 2):
        wait(f"xo{k}")
        wait(f"xp{k}")
    send("xs1", XB.at[0, pl.ds(1, 2)], XB.at[1, pl.ds(1, 2)], dc=1)
    for k in (6, 7):
        wait(f"xo{k}")
        wait(f"xp{k}")
    send("xs6", XB.at[0, pl.ds(6, 2)], XB.at[1, pl.ds(6, 2)], dc=1)
    for k in FAR:
        wait(f"xq{k}")
    send("xs3", XB.at[0, pl.ds(3, 3)], XB.at[1, pl.ds(3, 3)], dc=1)
    for k in (1, 7):
        wait(f"ty{k}")
    for k in (0, 1, 6, 3):
        wait(f"xs{k}")

    temp_row = jnp.exp(jnp.full((1, 512), log_temp_ref[0], F32))
    shift = bias_ref[0]
    col = lax.broadcasted_iota(jnp.int32, (1, 512), 1)
    col_core = (c + (col >> 8)) & 1
    col_x = (x + ((col >> 5) & 7)) & 7
    col_zl = (zl + ((col >> 4) & 1)) & 1
    col_id = ((y * NZ + zh) * 2 + col_core) * 256 + (col_x * 2 + col_zl) * ROWS + (col & 15)
    row = lax.broadcasted_iota(jnp.int32, (128, 1), 0)
    parts = [jnp.zeros((1, 512), F32) for _ in range(3)]

    def text_product(first):
        cols_x = XB[...].reshape(512, width)
        dy = jnp.dot(GT[pl.ds(first * 64, 128)], cols_x, preferred_element_type=F32).reshape(2, NZ, ROWS, width)
        DYF[pl.ds(first, 2)] = dy
        DYB[pl.ds(first, 2)] = dy.astype(BF16)

    def send_dy(first):
        for k in (first, first + 1):
            for r in LAST_Z.get(k, ()):
                send(f"dz{k}{r}", DYB.at[k, r], RZ1.at[k, r], dz=r)
        for k in (first, first + 1):
            if k in LAST_Y:
                r, n = LAST_Y[k]
                send(f"dy{k}", DYB.at[k, pl.ds(r, n)], RY.at[k, pl.ds(r, n)], dy=k)

    for first in (0, 6, 2, 4):
        for k in (first, first + 1):
            if k in (2, 3, 5, 6):
                wait(f"tp{k}")
            for r in LAST_Z.get(k, ()):
                wait(f"tw{k}{r}")
        row_y = (y + first + (row >> 6)) & 7
        row_zh = (zh + ((row >> 4) & 3)) & 3
        row_id = (x * 2 + zl) * 1024 + ((row_y * NZ + row_zh) * 2 + c) * ROWS + (row & 15)
        rows_y = YB[pl.ds(first, 2)].reshape(128, width)
        cols_x = XB[...].reshape(512, width)
        dots = lax.dot_general(rows_y, cols_x, (((1,), (1,)), ((), ())), preferred_element_type=F32)
        logits = temp_row * dots + shift
        match = row_id == col_id
        signed = jnp.where(match, -logits, logits)
        decay = jnp.exp(-jnp.abs(signed))
        loss = jnp.maximum(signed, 0.0) + jnp.log1p(decay)
        sig = jnp.where(signed >= 0, 1.0, decay) / (1.0 + decay)
        grad = jnp.where(match, -sig, sig)
        for n, value in enumerate((loss, grad * dots, grad)):
            parts[n] = parts[n] + jnp.sum(value, axis=0, keepdims=True)
        GT[pl.ds(first * 64, 128)] = grad.astype(BF16)
        if first != 4:
            text_product(first)
            send_dy(first)

    folded = [part[:, 0:128] + part[:, 128:256] + part[:, 256:384] + part[:, 384:512] for part in parts]
    PA[0] = jnp.concatenate(folded + [jnp.zeros((5, 128), F32)], axis=0)

    text_product(4)
    send_dy(4)
    texts_all = YB[...].reshape(512, width)
    over_texts = (((0,), (0,)), ((), ()))
    DXS[...] = lax.dot_general(GT[:, 256:512], texts_all, over_texts, preferred_element_type=F32).reshape(NX, 2, ROWS, width)
    for k, n in ((3, 3), (1, 2), (6, 2), (0, 1)):
        send(f"sx{k}", DXS.at[pl.ds(k, n)], RXS.at[pl.ds(k, n)], dc=1)
    DX0[...] = lax.dot_general(GT[:, 0:256], texts_all, over_texts, preferred_element_type=F32).reshape(NX, 2, ROWS, width)
    for j in FAR_FIRST:
        send(f"pa{NX - j}", PA.at[0], PA.at[NX - j], dx=j)
    for k in (1, 7):
        send(f"do{k}", DYB.at[k, 0], RY.at[k, 0], dy=k)
    for k, n in ((3, 3), (1, 2), (6, 2), (0, 1)):
        wait(f"sx{k}")
        both = DX0[pl.ds(k, n)] + RXS[pl.ds(k, n)]
        DX0[pl.ds(k, n)] = both
        DXB[pl.ds(k, n)] = both.astype(BF16)
        if k == 3:
            send("dl", DXB.at[pl.ds(3, 3), 1], RXL, dl=1)
        elif k:
            for j in (k, k + 1):
                send(f"dx{j}", DXB.at[j], RX.at[j], dx=j)

    def wide(ref):
        return ref.astype(F32)

    for k in range(1, NX):
        wait(f"pa{k}")
    total = PA[(0 - x) % NX]
    for a in range(1, NX):
        total = total + PA[(a - x) % NX]
    PB[0] = total
    for j in FAR_FIRST:
        send(f"pb{NY - j}", PB.at[0], PB.at[NY - j], dy=j)

    wait("dl")
    for n, k in enumerate(FAR):
        DXB[k, 0] = (DX0[k, 0] + wide(RXL[n])).astype(BF16)
        send(f"ex{k}", DXB.at[k, 0], RX2.at[n], dx=k)

    for n, (k, rows) in enumerate(LAST_Z.items()):
        part = DYF[k, 0]
        for r in rows:
            wait(f"dz{k}{r}")
            part = part + wide(RZ1[k, r])
        DYB[k, 0] = part.astype(BF16)
        send(f"ey{k}", DYB.at[k, 0], RY1.at[n], dy=k)

    for k in range(1, NY):
        wait(f"pb{k}")
    total = PB[(0 - y) % NY]
    for a in range(1, NY):
        total = total + PB[(a - y) % NY]
    PC[0] = total
    for to in others:
        m, a, b = to["dz"], to["dl"], to["dc"]
        slot = ((NZ - m) % NZ) * 4 + a * 2 + b
        send(f"pc{slot}", PC.at[0], PC.at[slot], **to)

    for k in NEAR:
        wait(f"dx{k}")
    part = DX0[0, 1]
    for k in NEAR:
        part = part + wide(RX[k, 1])
    DXB[0, 1] = part.astype(BF16)
    send("el", DXB.at[0, 1], RXZ, dl=1)

    for k in LAST_Y:
        wait(f"dy{k}")
    for r in (2, 1, 3):
        part = DYF[0, r]
        for k, (low, n) in LAST_Y.items():
            if low <= r < low + n:
                part = part + wide(RY[k, r])
        DYB[0, r] = part.astype(BF16)
        send(f"ez{r}", DYB.at[0, r], RZ.at[r - 1], dz=r)

    part = DYF[0, 0]
    for k in (1, 7):
        wait(f"do{k}")
        part = part + wide(RY[k, 0])
    DYO[...] = part
    part = DX0[0, 0]
    for k in NEAR:
        part = part + wide(RX[k, 0])
    DX0[0, 0] = part

    scale = jnp.exp(jnp.full((1, width), log_temp_ref[0], F32))
    x_norm, inv_x = normalize(images_ref[...])
    wait("el")
    part = DX0[0, 0] + wide(RXZ[...])
    for n, k in enumerate(FAR):
        wait(f"ex{k}")
        part = part + wide(RX2[n])
    grad_images_ref[...] = unnormalize(x_norm, inv_x, scale * part)

    y_norm, inv_y = normalize(texts_ref[...])
    part = DYO[...]
    for r in (1, 3, 2):
        wait(f"ez{r}")
        part = part + wide(RZ[r - 1])
    for n, k in enumerate(LAST_Z):
        wait(f"ey{k}")
        part = part + wide(RY1[n])
    grad_texts_ref[...] = unnormalize(y_norm, inv_y, scale * part)

    for slot in range(1, 16):
        wait(f"pc{slot}")
    total = None
    for m in range(NZ):
        for a in (0, 1):
            for b in (0, 1):
                term = PC[((m - zh) % NZ) * 4 + ((a - zl) % 2) * 2 + (b - c) % 2]
                total = term if total is None else total + term
    batch = float(images_ref.shape[0] * NX * NY * NZ * 4)
    temp = jnp.exp(jnp.full((1, 128), log_temp_ref[0], F32))
    sums_ref[...] = jnp.concatenate([total[0:1], temp * total[1:2], total[2:8]], axis=0) / batch

    for copy in sent.values():
        copy.wait_send()


def finish(
    grad_images_ref, grad_texts_ref, sums_ref,
    loss_out, grad_images_out, grad_texts_out, grad_temp_out, grad_bias_out,
    loss_ref, grad_temp_ref, grad_bias_ref, sems,
):
    copies = [
        pltpu.make_async_copy(src, dst, sems.at[n])
        for n, (src, dst) in enumerate(
            (
                (grad_images_ref, grad_images_out), (grad_texts_ref, grad_texts_out),
                (loss_ref, loss_out), (grad_temp_ref, grad_temp_out), (grad_bias_ref, grad_bias_out),
            )
        )
    ]
    for copy in copies[:2]:
        copy.start()
    loss_ref[0] = jnp.sum(sums_ref[0:1])
    grad_temp_ref[0] = jnp.sum(sums_ref[1:2])
    grad_bias_ref[0] = jnp.sum(sums_ref[2:3])
    for copy in copies[2:]:
        copy.start()
    for copy in copies:
        copy.wait()


def body(images, texts, log_temp, bias):
    rows, width = images.shape
    smem = pl.BlockSpec(memory_space=pltpu.SMEM)
    anywhere = pl.BlockSpec(memory_space=pl.ANY)
    scalar = jax.ShapeDtypeStruct((1,), F32)
    vmem = pl.BlockSpec(memory_space=pltpu.VMEM)
    wide = jax.ShapeDtypeStruct((rows, width), F32)
    piece = (rows, width)
    scratch = [
        ((2, NX, 2) + piece, BF16),
        ((NY, NZ) + piece, BF16),
        ((512, 512), BF16),
        ((NY, NZ) + piece, F32),
        ((NY, NZ) + piece, BF16),
        ((NY, NZ) + piece, BF16),
        ((7, NZ) + piece, BF16),
        ((5,) + piece, BF16),
        ((3,) + piece, BF16),
        (piece, F32),
        ((NX, 2) + piece, F32),
        ((NX, 2) + piece, F32),
        ((NX, 2) + piece, F32),
        ((NX, 2) + piece, BF16),
        ((NX, 2) + piece, BF16),
        ((3,) + piece, BF16),
        ((3,) + piece, BF16),
        (piece, BF16),
        ((NX, 8, 128), F32),
        ((NY, 8, 128), F32),
        ((16, 8, 128), F32),
    ]
    dma = pltpu.SemaphoreType.DMA
    grad_images, grad_texts, sums = pl.pallas_call(
        kernel,
        out_shape=(wide, wide, jax.ShapeDtypeStruct((8, 128), F32)),
        in_specs=[smem, smem, vmem, vmem],
        out_specs=(vmem, vmem, vmem),
        scratch_shapes=[pltpu.VMEM(shape, kind) for shape, kind in scratch] + [dma((128,)), dma((128,))],
        compiler_params=pltpu.CompilerParams(collective_id=0, has_side_effects=True, vmem_limit_bytes=VMEM_LIMIT),
        name="sigmoid_loss",
    )(log_temp, bias, images, texts)
    return pl.pallas_call(
        finish,
        out_shape=(scalar, wide, wide, scalar, scalar),
        in_specs=[vmem] * 3,
        out_specs=(anywhere,) * 5,
        scratch_shapes=[pltpu.SMEM((1,), F32)] * 3 + [dma((5,))],
        compiler_params=pltpu.CompilerParams(vmem_limit_bytes=2**20),
        name="write_out",
    )(grad_images, grad_texts, sums)


def solution(mesh):
    in_specs = (P(("img", "txt"), None), P(("txt", "img"), None), P(), P())
    out_specs = (P(), P(("img", "txt"), None), P(("txt", "img"), None), P(), P())
    return jax.shard_map(body, mesh=mesh, in_specs=in_specs, out_specs=out_specs, check_vma=False)
```

time: 385 us -> 70 us (0.18)
  waiting for transfers between devices: 194 us -> 0 us
  blocking collectives: 144 us -> 0 us
  Pallas kernels: 0 us -> 66.2 us
  between operations: 20.5 us -> 1.94 us
  other arithmetic: 11.5 us -> 0 us
  matrix products: 9.75 us -> 0 us
    reduce_scatter x2 -> x0, waiting for transfers between devices: 120 us -> none  [the longest x1 120 us: body(): lax.psum_scatter(temp * jnp.dot(grad_low.T, x_block, preferred_element_ty...]
    psum x1 -> x0, blocking collectives: 112 us -> none  [body(): totals = lax.psum(partials, ('img', 'txt'))]
    all_gather x1 -> x0, waiting for transfers between devices: 73.6 us -> none  [body(): lax.all_gather(y_norm.astype(jnp.bfloat16), 'img', axis=0, tiled=True)]
    pallas_call x0 -> x2, Pallas kernels: none -> 66.2 us  [the longest x1 65.5 us: body(): pl.pallas_call(kernel, out_shape=(wide, wide, jax.ShapeDtypeStruct((8, 12...]
    all_gather x1 -> x0, blocking collectives: 32.2 us -> none  [body(): lax.all_gather(x_norm.astype(jnp.bfloat16), 'txt', axis=0, tiled=True)]
    dot_general x3 -> x0, matrix products: 9.75 us -> none  [the longest x1 4.28 us: body(): dots = jnp.dot(x_block, y_block.T, preferred_element_type=jnp.float32)]
    reduce_sum x4 -> x0, other arithmetic: 3.93 us -> none  [the longest x2 2.15 us: unnormalize(): inner = jnp.sum(normed * grad_normed, axis=-1, keepdims=True)]
  transfers between devices with their start and end apart: 3 -> 0, of which waited for: 2 -> 0; matrix products, arithmetic and copies ran while one was open for 3% -> 0% of each run, Pallas kernels for 0% -> 0%
where the time goes in v2:
time: 70 us; the launch traced here: 69.7 us
  Pallas kernels  66.2 us (95%)
  between operations  1.94 us (3%)
  local copies, waits for them, and re-layouts  1.53 us (2%)
    pallas_call x1, Pallas kernels, body(): pl.pallas_call(kernel, out_shape=(wide, wide, jax.ShapeDtypeStruct((8, 12...  65.5 us
    unnamed x4, local copies, waits for them, and re-layouts  1.53 us

profile of v2, /device:TPU:1, one launch (start us, length us, event | category | flops | bytes accessed | tf_op | source)
XLA Modules:
  0.0 69.7 jit_solution(8731608377389230124)
XLA Ops:
  1.9 0.0 copy-start
  1.9 0.8 %copy-done = bf16[16,1152]{1,0:T(8,128)(2,1)S(1)} copy-done((bf16[16,1152]{1,0:T(8,128)(2,1)S(1)}, bf16[16,1152]{1,0:T(8,128)(2,1)}, u32[]{:S(2)}) %copy-start) | copy-done | bytes 36888
  2.7 0.0 copy-start.1
  2.7 0.8 %copy-done.1 = bf16[16,1152]{1,0:T(8,128)(2,1)S(1)} copy-done((bf16[16,1152]{1,0:T(8,128)(2,1)S(1)}, bf16[16,1152]{1,0:T(8,128)(2,1)}, u32[]{:S(2)}) %copy-start.1) | copy-done | bytes 36888
  3.5 65.5 %sigmoid_loss.1 = (f32[16,1152]{1,0:T(8,128)S(1)}, f32[16,1152]{1,0:T(8,128)S(1)}, f32[8,128]{1,0:T(8,128)S(1)}) custom-call(f32[1]{0:T(128)S(6)} %copy.9.log_temp_ref, f32[1]{0:T(128)S(6)} %copy.10.bias_ref, bf16[16,1152]{1,0:T(8,128)(2,1)S(1)} %copy-done, bf16[16,1152]{1,0:T(8,128)(2,1)S(1)} %copy-done.1), custom_call_target="tpu_custom_call" | custom-call | tf_op jit(solution)/shard_map/sigmoid_loss/pallas_call | solution.py:348
  68.9 0.7 %write_out.1 = (f32[1]{0:T(128)}, f32[16,1152]{1,0:T(8,128)}, f32[16,1152]{1,0:T(8,128)}, f32[1]{0:T(128)}, f32[1]{0:T(128)}) custom-call(f32[16,1152]{1,0:T(8,128)S(1)} %get-tuple-element.8.grad_images_ref, f32[16,1152]{1,0:T(8,128)S(1)} %get-tuple-element.9.grad_texts_ref, f32[8,128]{1,0:T(8,128)S(1)} %get-tuple-element.10.sums_ref), custom_call_target="tpu_custom_call" | custom-call | tf_op jit(solution)/shard_map/write_out/pallas_call | solution.py:357
Async XLA Ops:
  1.9 0.8 %copy-start = (bf16[16,1152]{1,0:T(8,128)(2,1)S(1)}, bf16[16,1152]{1,0:T(8,128)(2,1)}, u32[]{:S(2)}) copy-start(bf16[16,1152]{1,0:T(8,128)(2,1)} %images_ref.1) | copy-start | bytes 110596
  2.7 0.8 %copy-start.1 = (bf16[16,1152]{1,0:T(8,128)(2,1)S(1)}, bf16[16,1152]{1,0:T(8,128)(2,1)}, u32[]{:S(2)}) copy-start(bf16[16,1152]{1,0:T(8,128)(2,1)} %texts_ref.1) | copy-start | bytes 110596

commit v3 on v2

--- a/solution.py
+++ b/solution.py
@@ -12,10 +12,11 @@
 VMEM_LIMIT = 48 * 2**20
 FAR_FIRST = (4, 3, 5, 2, 6, 1, 7)
 NEAR_FIRST = (1, 7, 2, 6, 3, 5, 4)
-LAST_Z = {4: (1, 3, 2), 3: (1, 3), 5: (1, 3), 2: (1,), 6: (3,)}
-LAST_Y = {1: (1, 3), 7: (1, 3), 3: (2, 1), 5: (2, 1), 2: (2, 2), 6: (1, 2)}
+LAST_Z = {4: (1, 3, 2), 3: (1, 3), 5: (1, 3)}
+LAST_Y = {1: (1, 3), 7: (1, 3), 3: (2, 1), 5: (2, 1), 2: (1, 3), 6: (1, 3)}
 FAR = (3, 4, 5)
-NEAR = (1, 7, 2, 6)
+NEAR = (2, 6, 1, 7)
+ALONG_X = (3, 5, 2, 6, 1, 7)
 
 
 def normalize(embed):
@@ -30,15 +31,16 @@
 
 
 def kernel(
-    log_temp_ref, bias_ref, images_ref, texts_ref,
+    given_ref,
     grad_images_ref, grad_texts_ref, sums_ref,
-    XB, YB, GT, DYF, DYB, RY, RZ1, RY1, RZ, DYO, DXS, RXS, DX0, DXB, RX, RXL, RX2, RXZ, PA, PB, PC,
+    XB, YB, GT, DYF, DYB, RY, RZ1, RY1, RZ, DYO, DXS, RXS, DX0, DXB, RX, RXL, RXZ, PA, PB, PC,
     ss, rs,
 ):
     img, txt = lax.axis_index("img"), lax.axis_index("txt")
     y, zh, c = img // (NZ * 2), (img // 2) % NZ, img % 2
     x, zl = txt // 2, txt % 2
-    width = images_ref.shape[1]
+    width = given_ref.shape[1]
+    images_ref, texts_ref = given_ref.at[0:ROWS], given_ref.at[ROWS : 2 * ROWS]
 
     def device(dx=0, dy=0, dz=0, dl=0, dc=0):
         i = ((((y + dy) % NY) * NZ + (zh + dz) % NZ) * 2) + (c + dc) % 2
@@ -58,6 +60,14 @@
     def wait(name):
         sent[name].wait_recv()
 
+    drained = set()
+
+    def drain(*kinds):
+        for name, copy in sent.items():
+            if name not in drained and name.startswith(kinds):
+                drained.add(name)
+                copy.wait_send()
+
     others = [dict(dz=m, dl=a, dc=b) for m in range(NZ) for a in (0, 1) for b in (0, 1) if (m, a, b) != (0, 0, 0)]
     peers = [dict(dx=j) for j in range(1, NX)] + [dict(dy=j) for j in range(1, NY)] + others
     barrier = pltpu.get_barrier_semaphore()
@@ -73,25 +83,33 @@
     for m in (1, 3, 2):
         send(f"tz{NZ - m}", YB.at[0, 0], YB.at[0, NZ - m], dz=m)
     send("xl", XB.at[0, 0, 0], XB.at[0, 0, 1], dl=1)
-    for j in FAR_FIRST:
+    for j in (6, 2, 4):
         send(f"ty{NY - j}", YB.at[0, 0], YB.at[NY - j, 0], dy=j)
+    for j in (4, 3, 5):
+        send(f"xo{NX - j}", XB.at[0, 0, 0], XB.at[0, NX - j, 0], dx=j)
+    for j in (1, 7):
+        send(f"ty{NY - j}", YB.at[0, 0], YB.at[NY - j, 0], dy=j)
+    for j in (2, 6, 1, 7):
         send(f"xo{NX - j}", XB.at[0, 0, 0], XB.at[0, NX - j, 0], dx=j)
     wait("xl")
     for k in (2, 6, 1, 7):
         send(f"xp{k}", XB.at[0, 0, 1], XB.at[0, k, 1], dx=NX - k)
+    for k, near, to in ((3, 2, NY - 1), (5, 6, 1)):
+        wait(f"ty{near}")
+        send(f"ty{k}", YB.at[near, 0], YB.at[k, 0], dy=to)
     for r in (1, 3, 2):
         wait(f"tz{r}")
     for k in (1, 7, 3, 5):
         r, n = LAST_Y[k]
         send(f"tp{k}", YB.at[0, pl.ds(r, n)], YB.at[k, pl.ds(r, n)], dy=NY - k)
     send("xs0", XB.at[0, 0], XB.at[1, 0], dc=1)
-    for k, rs_of in LAST_Z.items():
+    for k in (4, 3, 5):
+        wait(f"xo{k}")
+        send(f"xq{k}", XB.at[0, k, 0], XB.at[0, k, 1], dl=1)
+    for k, rows in LAST_Z.items():
         wait(f"ty{k}")
-        for r in rs_of:
+        for r in rows:
             send(f"tw{k}{r}", YB.at[k, 0], YB.at[k, r], dz=NZ - r)
-        if k in FAR:
-            wait(f"xo{k}")
-            send(f"xq{k}", XB.at[0, k, 0], XB.at[0, k, 1], dl=1)
     for k, near, to in ((2, 1, NY - 1), (6, 7, 1)):
         r, n = LAST_Y[k]
         wait(f"tp{near}")
@@ -112,8 +130,8 @@
     for k in (0, 1, 6, 3):
         wait(f"xs{k}")
 
-    temp_row = jnp.exp(jnp.full((1, 512), log_temp_ref[0], F32))
-    shift = bias_ref[0]
+    temp_row = jnp.exp(given_ref[2 * ROWS : 2 * ROWS + 1, 0:512])
+    shift_row = given_ref[2 * ROWS + 1 : 2 * ROWS + 2, 0:512]
     col = lax.broadcasted_iota(jnp.int32, (1, 512), 1)
     col_core = (c + (col >> 8)) & 1
     col_x = (x + ((col >> 5) & 7)) & 7
@@ -137,7 +155,7 @@
                 r, n = LAST_Y[k]
                 send(f"dy{k}", DYB.at[k, pl.ds(r, n)], RY.at[k, pl.ds(r, n)], dy=k)
 
-    for first in (0, 6, 2, 4):
+    for first in (0, 4, 2, 6):
         for k in (first, first + 1):
             if k in (2, 3, 5, 6):
                 wait(f"tp{k}")
@@ -149,7 +167,7 @@
         rows_y = YB[pl.ds(first, 2)].reshape(128, width)
         cols_x = XB[...].reshape(512, width)
         dots = lax.dot_general(rows_y, cols_x, (((1,), (1,)), ((), ())), preferred_element_type=F32)
-        logits = temp_row * dots + shift
+        logits = temp_row * dots + shift_row
         match = row_id == col_id
         signed = jnp.where(match, -logits, logits)
         decay = jnp.exp(-jnp.abs(signed))
@@ -159,38 +177,44 @@
         for n, value in enumerate((loss, grad * dots, grad)):
             parts[n] = parts[n] + jnp.sum(value, axis=0, keepdims=True)
         GT[pl.ds(first * 64, 128)] = grad.astype(BF16)
-        if first != 4:
+        if first != 6:
             text_product(first)
             send_dy(first)
 
     folded = [part[:, 0:128] + part[:, 128:256] + part[:, 256:384] + part[:, 384:512] for part in parts]
     PA[0] = jnp.concatenate(folded + [jnp.zeros((5, 128), F32)], axis=0)
 
-    text_product(4)
-    send_dy(4)
     texts_all = YB[...].reshape(512, width)
     over_texts = (((0,), (0,)), ((), ()))
-    DXS[...] = lax.dot_general(GT[:, 256:512], texts_all, over_texts, preferred_element_type=F32).reshape(NX, 2, ROWS, width)
-    for k, n in ((3, 3), (1, 2), (6, 2), (0, 1)):
-        send(f"sx{k}", DXS.at[pl.ds(k, n)], RXS.at[pl.ds(k, n)], dc=1)
-    DX0[...] = lax.dot_general(GT[:, 0:256], texts_all, over_texts, preferred_element_type=F32).reshape(NX, 2, ROWS, width)
+    groups = ((4, 4), (0, 4))
+    for first, n in groups:
+        rows = pl.ds(256 + first * 32, n * 32)
+        DXS[pl.ds(first, n)] = lax.dot_general(
+            GT[:, rows], texts_all, over_texts, preferred_element_type=F32
+        ).reshape(n, 2, ROWS, width)
+        send(f"sx{first}", DXS.at[pl.ds(first, n)], RXS.at[pl.ds(first, n)], dc=1)
+    text_product(6)
+    send_dy(6)
     for j in FAR_FIRST:
         send(f"pa{NX - j}", PA.at[0], PA.at[NX - j], dx=j)
-    for k in (1, 7):
-        send(f"do{k}", DYB.at[k, 0], RY.at[k, 0], dy=k)
-    for k, n in ((3, 3), (1, 2), (6, 2), (0, 1)):
-        wait(f"sx{k}")
-        both = DX0[pl.ds(k, n)] + RXS[pl.ds(k, n)]
-        DX0[pl.ds(k, n)] = both
-        DXB[pl.ds(k, n)] = both.astype(BF16)
-        if k == 3:
-            send("dl", DXB.at[pl.ds(3, 3), 1], RXL, dl=1)
-        elif k:
-            for j in (k, k + 1):
-                send(f"dx{j}", DXB.at[j], RX.at[j], dx=j)
+    DX0[...] = lax.dot_general(GT[:, 0:256], texts_all, over_texts, preferred_element_type=F32).reshape(NX, 2, ROWS, width)
+    for first, n in groups:
+        wait(f"sx{first}")
+        both = DX0[pl.ds(first, n)] + RXS[pl.ds(first, n)]
+        DX0[pl.ds(first, n)] = both
+        DXB[pl.ds(first, n)] = both.astype(BF16)
+        for k in range(first, first + n):
+            if k == 4:
+                send("dl", DXB.at[4, 1], RXL, dl=1)
+            elif k:
+                send(f"dp{k}", DXB.at[k, 1], RX.at[k, 1], dx=k)
+    for k in ALONG_X:
+        send(f"dx{k}", DXB.at[k, 0], RX.at[k, 0], dx=k)
 
     def wide(ref):
         return ref.astype(F32)
+
+    drain("t", "xl", "xo", "xp", "xq", "xs")
 
     for k in range(1, NX):
         wait(f"pa{k}")
@@ -198,13 +222,10 @@
     for a in range(1, NX):
         total = total + PA[(a - x) % NX]
     PB[0] = total
-    for j in FAR_FIRST:
-        send(f"pb{NY - j}", PB.at[0], PB.at[NY - j], dy=j)
-
-    wait("dl")
-    for n, k in enumerate(FAR):
-        DXB[k, 0] = (DX0[k, 0] + wide(RXL[n])).astype(BF16)
-        send(f"ex{k}", DXB.at[k, 0], RX2.at[n], dx=k)
+    for to in others:
+        m, a, b = to["dz"], to["dl"], to["dc"]
+        slot = ((NZ - m) % NZ) * 4 + a * 2 + b
+        send(f"pb{slot}", PB.at[0], PB.at[slot], **to)
 
     for n, (k, rows) in enumerate(LAST_Z.items()):
         part = DYF[k, 0]
@@ -214,24 +235,12 @@
         DYB[k, 0] = part.astype(BF16)
         send(f"ey{k}", DYB.at[k, 0], RY1.at[n], dy=k)
 
-    for k in range(1, NY):
-        wait(f"pb{k}")
-    total = PB[(0 - y) % NY]
-    for a in range(1, NY):
-        total = total + PB[(a - y) % NY]
-    PC[0] = total
-    for to in others:
-        m, a, b = to["dz"], to["dl"], to["dc"]
-        slot = ((NZ - m) % NZ) * 4 + a * 2 + b
-        send(f"pc{slot}", PC.at[0], PC.at[slot], **to)
-
     for k in NEAR:
-        wait(f"dx{k}")
-    part = DX0[0, 1]
-    for k in NEAR:
-        part = part + wide(RX[k, 1])
-    DXB[0, 1] = part.astype(BF16)
-    send("el", DXB.at[0, 1], RXZ, dl=1)
+        send(f"do{k}", DYB.at[k, 0], RY.at[k, 0], dy=k)
+
+    wait("dl")
+    DXB[4, 0] = (DX0[4, 0] + wide(RXL[...])).astype(BF16)
+    send("ex", DXB.at[4, 0], RX.at[4, 0], dx=4)
 
     for k in LAST_Y:
         wait(f"dy{k}")
@@ -243,25 +252,40 @@
         DYB[0, r] = part.astype(BF16)
         send(f"ez{r}", DYB.at[0, r], RZ.at[r - 1], dz=r)
 
+    drain("dz", "dy", "sx", "pa")
+
+    part = DX0[0, 1]
+    for k in ALONG_X:
+        wait(f"dp{k}")
+        part = part + wide(RX[k, 1])
+    DXB[0, 1] = part.astype(BF16)
+    send("el", DXB.at[0, 1], RXZ, dl=1)
+
+    for slot in range(1, 16):
+        wait(f"pb{slot}")
+    total = None
+    for m in range(NZ):
+        for a in (0, 1):
+            for b in (0, 1):
+                term = PB[((m - zh) % NZ) * 4 + ((a - zl) % 2) * 2 + (b - c) % 2]
+                total = term if total is None else total + term
+    PC[0] = total
+    for j in FAR_FIRST:
+        send(f"pc{NY - j}", PC.at[0], PC.at[NY - j], dy=j)
+
     part = DYF[0, 0]
-    for k in (1, 7):
+    for k in NEAR:
         wait(f"do{k}")
         part = part + wide(RY[k, 0])
     DYO[...] = part
     part = DX0[0, 0]
-    for k in NEAR:
+    for k in ALONG_X:
+        wait(f"dx{k}")
         part = part + wide(RX[k, 0])
     DX0[0, 0] = part
 
-    scale = jnp.exp(jnp.full((1, width), log_temp_ref[0], F32))
-    x_norm, inv_x = normalize(images_ref[...])
-    wait("el")
-    part = DX0[0, 0] + wide(RXZ[...])
-    for n, k in enumerate(FAR):
-        wait(f"ex{k}")
-        part = part + wide(RX2[n])
-    grad_images_ref[...] = unnormalize(x_norm, inv_x, scale * part)
-
+    drain("pb", "dp", "dx", "dl", "do", "ey", "ex")
+    scale = jnp.exp(given_ref[2 * ROWS : 2 * ROWS + 1])
     y_norm, inv_y = normalize(texts_ref[...])
     part = DYO[...]
     for r in (1, 3, 2):
@@ -272,20 +296,23 @@
         part = part + wide(RY1[n])
     grad_texts_ref[...] = unnormalize(y_norm, inv_y, scale * part)
 
-    for slot in range(1, 16):
-        wait(f"pc{slot}")
-    total = None
-    for m in range(NZ):
-        for a in (0, 1):
-            for b in (0, 1):
-                term = PC[((m - zh) % NZ) * 4 + ((a - zl) % 2) * 2 + (b - c) % 2]
-                total = term if total is None else total + term
-    batch = float(images_ref.shape[0] * NX * NY * NZ * 4)
-    temp = jnp.exp(jnp.full((1, 128), log_temp_ref[0], F32))
+    x_norm, inv_x = normalize(images_ref[...])
+    wait("el")
+    part = DX0[0, 0] + wide(RXZ[...])
+    wait("ex")
+    part = part + wide(RX[4, 0])
+    grad_images_ref[...] = unnormalize(x_norm, inv_x, scale * part)
+
+    for k in range(1, NY):
+        wait(f"pc{k}")
+    total = PC[(0 - y) % NY]
+    for a in range(1, NY):
+        total = total + PC[(a - y) % NY]
+    batch = float(ROWS * NX * NY * NZ * 4)
+    temp = jnp.exp(given_ref[2 * ROWS : 2 * ROWS + 1, 0:128])
     sums_ref[...] = jnp.concatenate([total[0:1], temp * total[1:2], total[2:8]], axis=0) / batch
 
-    for copy in sent.values():
-        copy.wait_send()
+    drain("")
 
 
 def finish(
@@ -315,7 +342,6 @@
 
 def body(images, texts, log_temp, bias):
     rows, width = images.shape
-    smem = pl.BlockSpec(memory_space=pltpu.SMEM)
     anywhere = pl.BlockSpec(memory_space=pl.ANY)
     scalar = jax.ShapeDtypeStruct((1,), F32)
     vmem = pl.BlockSpec(memory_space=pltpu.VMEM)
@@ -328,8 +354,8 @@
         ((NY, NZ) + piece, F32),
         ((NY, NZ) + piece, BF16),
         ((NY, NZ) + piece, BF16),
-        ((7, NZ) + piece, BF16),
-        ((5,) + piece, BF16),
+        ((6, NZ) + piece, BF16),
+        ((3,) + piece, BF16),
         ((3,) + piece, BF16),
         (piece, F32),
         ((NX, 2) + piece, F32),
@@ -337,23 +363,24 @@
         ((NX, 2) + piece, F32),
         ((NX, 2) + piece, BF16),
         ((NX, 2) + piece, BF16),
-        ((3,) + piece, BF16),
-        ((3,) + piece, BF16),
+        (piece, BF16),
         (piece, BF16),
         ((NX, 8, 128), F32),
+        ((16, 8, 128), F32),
         ((NY, 8, 128), F32),
-        ((16, 8, 128), F32),
     ]
     dma = pltpu.SemaphoreType.DMA
+    scalars = jnp.concatenate([jnp.broadcast_to(v[0], (1, width)) for v in (log_temp, bias)] + [jnp.zeros((6, width), F32)])
+    given = jnp.concatenate([images.astype(F32), texts.astype(F32), scalars])
     grad_images, grad_texts, sums = pl.pallas_call(
         kernel,
         out_shape=(wide, wide, jax.ShapeDtypeStruct((8, 128), F32)),
-        in_specs=[smem, smem, vmem, vmem],
+        in_specs=[vmem],
         out_specs=(vmem, vmem, vmem),
         scratch_shapes=[pltpu.VMEM(shape, kind) for shape, kind in scratch] + [dma((128,)), dma((128,))],
         compiler_params=pltpu.CompilerParams(collective_id=0, has_side_effects=True, vmem_limit_bytes=VMEM_LIMIT),
         name="sigmoid_loss",
-    )(log_temp, bias, images, texts)
+    )(given)
     return pl.pallas_call(
         finish,
         out_shape=(scalar, wide, wide, scalar, scalar),

time: 70 us -> 66.4 us (0.949)
  Pallas kernels: 66.2 us -> 63.3 us
  local copies, waits for them, and re-layouts: 1.53 us -> 0.83 us
    pallas_call x1, Pallas kernels: 65.5 us -> 62.6 us  [body(): pl.pallas_call(kernel, out_shape=(wide, wide, jax.ShapeDtypeStruct((8, 12...]
    unnamed x4 -> x2, local copies, waits for them, and re-layouts: 1.53 us -> 0.01 us
    concatenate x0 -> x1, local copies, waits for them, and re-layouts: none -> 0.82 us  [body(): given = jnp.concatenate([images.astype(F32), texts.astype(F32), scalars])]
where the time goes in v3:
time: 66.4 us; the launch traced here: 66.1 us
  Pallas kernels  63.3 us (95%)
  between operations  1.98 us (3%)
  local copies, waits for them, and re-layouts  0.83 us (1%)
    pallas_call x1, Pallas kernels, body(): pl.pallas_call(kernel, out_shape=(wide, wide, jax.ShapeDtypeStruct((8, 12...  62.6 us

profile of v3, /device:TPU:1, one launch (start us, length us, event | category | flops | bytes accessed | tf_op | source)
XLA Modules:
  0.0 66.1 jit_solution(8021132626060077574)
XLA Ops:
  0.6 0.0 copy-start
  2.0 0.0 copy-done
  2.0 0.8 %concatenate.3.given_ref = f32[40,1152]{1,0:T(8,128)S(1)} concatenate(bf16[16,1152]{1,0:T(8,128)(2,1)S(1)} %copy-done, bf16[16,1152]{1,0:T(8,128)(2,1)} %param.5, f32[1,1152]{1,0:T(1,128)S(1)} %broadcast_in_dim.9, f32[1,1152]{1,0:T(1,128)S(1)} %broadcast_in_dim.10, f32[6,1152]{1,0:T(8,128)S(1)} %broadcast_in_dim.11), dimensions={0} | concatenate | bytes 294912 | tf_op jit(solution)/shard_map/concatenate | solution.py:374
  2.8 62.6 %sigmoid_loss.1 = (f32[16,1152]{1,0:T(8,128)S(1)}, f32[16,1152]{1,0:T(8,128)S(1)}, f32[8,128]{1,0:T(8,128)S(1)}) custom-call(f32[40,1152]{1,0:T(8,128)S(1)} %concatenate.3.given_ref), custom_call_target="tpu_custom_call" | custom-call | tf_op jit(solution)/shard_map/sigmoid_loss/pallas_call | solution.py:375
  65.4 0.7 %write_out.1 = (f32[1]{0:T(128)}, f32[16,1152]{1,0:T(8,128)}, f32[16,1152]{1,0:T(8,128)}, f32[1]{0:T(128)}, f32[1]{0:T(128)}) custom-call(f32[16,1152]{1,0:T(8,128)S(1)} %get-tuple-element.8.grad_images_ref, f32[16,1152]{1,0:T(8,128)S(1)} %get-tuple-element.9.grad_texts_ref, f32[8,128]{1,0:T(8,128)S(1)} %get-tuple-element.10.sums_ref), custom_call_target="tpu_custom_call" | custom-call | tf_op jit(solution)/shard_map/write_out/pallas_call | solution.py:384
  (3 shorter events, 0.0 us)
Async XLA Ops:
  0.6 1.3 %copy-start = (bf16[16,1152]{1,0:T(8,128)(2,1)S(1)}, bf16[16,1152]{1,0:T(8,128)(2,1)}, u32[]{:S(2)}) copy-start(bf16[16,1152]{1,0:T(8,128)(2,1)} %param.4) | copy-start | bytes 110596

commit v4 on v3

--- a/solution.py
+++ b/solution.py
@@ -16,7 +16,6 @@
 LAST_Y = {1: (1, 3), 7: (1, 3), 3: (2, 1), 5: (2, 1), 2: (1, 3), 6: (1, 3)}
 FAR = (3, 4, 5)
 NEAR = (2, 6, 1, 7)
-ALONG_X = (3, 5, 2, 6, 1, 7)
 
 
 def normalize(embed):
@@ -99,9 +98,8 @@
         send(f"ty{k}", YB.at[near, 0], YB.at[k, 0], dy=to)
     for r in (1, 3, 2):
         wait(f"tz{r}")
-    for k in (1, 7, 3, 5):
-        r, n = LAST_Y[k]
-        send(f"tp{k}", YB.at[0, pl.ds(r, n)], YB.at[k, pl.ds(r, n)], dy=NY - k)
+        for k in (1, 7, 3, 5) if r == 2 else (1, 7):
+            send(f"tp{k}{r}", YB.at[0, r], YB.at[k, r], dy=NY - k)
     send("xs0", XB.at[0, 0], XB.at[1, 0], dc=1)
     for k in (4, 3, 5):
         wait(f"xo{k}")
@@ -111,9 +109,9 @@
         for r in rows:
             send(f"tw{k}{r}", YB.at[k, 0], YB.at[k, r], dz=NZ - r)
     for k, near, to in ((2, 1, NY - 1), (6, 7, 1)):
-        r, n = LAST_Y[k]
-        wait(f"tp{near}")
-        send(f"tp{k}", YB.at[near, pl.ds(r, n)], YB.at[k, pl.ds(r, n)], dy=to)
+        for r in (1, 3, 2):
+            wait(f"tp{near}{r}")
+            send(f"tp{k}{r}", YB.at[near, r], YB.at[k, r], dy=to)
     for k in (1, 2):
         wait(f"xo{k}")
         wait(f"xp{k}")
@@ -157,8 +155,8 @@
 
     for first in (0, 4, 2, 6):
         for k in (first, first + 1):
-            if k in (2, 3, 5, 6):
-                wait(f"tp{k}")
+            for r in {2: (1, 3, 2), 6: (1, 3, 2), 3: (2,), 5: (2,)}.get(k, ()):
+                wait(f"tp{k}{r}")
             for r in LAST_Z.get(k, ()):
                 wait(f"tw{k}{r}")
         row_y = (y + first + (row >> 6)) & 7
@@ -186,12 +184,9 @@
 
     texts_all = YB[...].reshape(512, width)
     over_texts = (((0,), (0,)), ((), ()))
-    groups = ((4, 4), (0, 4))
+    groups = ((3, 3), (1, 2), (6, 2), (0, 1))
+    DXS[...] = lax.dot_general(GT[:, 256:512], texts_all, over_texts, preferred_element_type=F32).reshape(NX, 2, ROWS, width)
     for first, n in groups:
-        rows = pl.ds(256 + first * 32, n * 32)
-        DXS[pl.ds(first, n)] = lax.dot_general(
-            GT[:, rows], texts_all, over_texts, preferred_element_type=F32
-        ).reshape(n, 2, ROWS, width)
         send(f"sx{first}", DXS.at[pl.ds(first, n)], RXS.at[pl.ds(first, n)], dc=1)
     text_product(6)
     send_dy(6)
@@ -203,18 +198,26 @@
         both = DX0[pl.ds(first, n)] + RXS[pl.ds(first, n)]
         DX0[pl.ds(first, n)] = both
         DXB[pl.ds(first, n)] = both.astype(BF16)
-        for k in range(first, first + n):
-            if k == 4:
-                send("dl", DXB.at[4, 1], RXL, dl=1)
-            elif k:
+        if first == 3:
+            send("dl", DXB.at[pl.ds(3, 3), 1], RXL, dl=1)
+        elif first:
+            for k in (first, first + 1):
                 send(f"dp{k}", DXB.at[k, 1], RX.at[k, 1], dx=k)
-    for k in ALONG_X:
+    for k in NEAR:
         send(f"dx{k}", DXB.at[k, 0], RX.at[k, 0], dx=k)
 
     def wide(ref):
         return ref.astype(F32)
 
     drain("t", "xl", "xo", "xp", "xq", "xs")
+
+    for n, (k, rows) in enumerate(LAST_Z.items()):
+        part = DYF[k, 0]
+        for r in rows:
+            wait(f"dz{k}{r}")
+            part = part + wide(RZ1[k, r])
+        DYB[k, 0] = part.astype(BF16)
+        send(f"ey{k}", DYB.at[k, 0], RY1.at[n], dy=k)
 
     for k in range(1, NX):
         wait(f"pa{k}")
@@ -227,20 +230,13 @@
         slot = ((NZ - m) % NZ) * 4 + a * 2 + b
         send(f"pb{slot}", PB.at[0], PB.at[slot], **to)
 
-    for n, (k, rows) in enumerate(LAST_Z.items()):
-        part = DYF[k, 0]
-        for r in rows:
-            wait(f"dz{k}{r}")
-            part = part + wide(RZ1[k, r])
-        DYB[k, 0] = part.astype(BF16)
-        send(f"ey{k}", DYB.at[k, 0], RY1.at[n], dy=k)
-
     for k in NEAR:
         send(f"do{k}", DYB.at[k, 0], RY.at[k, 0], dy=k)
 
     wait("dl")
-    DXB[4, 0] = (DX0[4, 0] + wide(RXL[...])).astype(BF16)
-    send("ex", DXB.at[4, 0], RX.at[4, 0], dx=4)
+    for n, k in enumerate(FAR):
+        DXB[k, 0] = (DX0[k, 0] + wide(RXL[n])).astype(BF16)
+        send(f"ex{k}", DXB.at[k, 0], RX.at[k, 0], dx=k)
 
     for k in LAST_Y:
         wait(f"dy{k}")
@@ -255,7 +251,7 @@
     drain("dz", "dy", "sx", "pa")
 
     part = DX0[0, 1]
-    for k in ALONG_X:
+    for k in NEAR:
         wait(f"dp{k}")
         part = part + wide(RX[k, 1])
     DXB[0, 1] = part.astype(BF16)
@@ -279,7 +275,7 @@
         part = part + wide(RY[k, 0])
     DYO[...] = part
     part = DX0[0, 0]
-    for k in ALONG_X:
+    for k in NEAR:
         wait(f"dx{k}")
         part = part + wide(RX[k, 0])
     DX0[0, 0] = part
@@ -299,8 +295,9 @@
     x_norm, inv_x = normalize(images_ref[...])
     wait("el")
     part = DX0[0, 0] + wide(RXZ[...])
-    wait("ex")
-    part = part + wide(RX[4, 0])
+    for k in FAR:
+        wait(f"ex{k}")
+        part = part + wide(RX[k, 0])
     grad_images_ref[...] = unnormalize(x_norm, inv_x, scale * part)
 
     for k in range(1, NY):
@@ -363,7 +360,7 @@
         ((NX, 2) + piece, F32),
         ((NX, 2) + piece, BF16),
         ((NX, 2) + piece, BF16),
-        (piece, BF16),
+        ((3,) + piece, BF16),
         (piece, BF16),
         ((NX, 8, 128), F32),
         ((16, 8, 128), F32),

time: 66.4 us -> 65.7 us (0.989)
  Pallas kernels: 63.3 us -> 62.5 us
    pallas_call x1, Pallas kernels: 62.6 us -> 61.8 us  [body(): pl.pallas_call(kernel, out_shape=(wide, wide, jax.ShapeDtypeStruct((8, 12...]
where the time goes in v4:
time: 65.7 us; the launch traced here: 65.3 us
  Pallas kernels  62.5 us (95%)
  between operations  1.98 us (3%)
  local copies, waits for them, and re-layouts  0.83 us (1%)
    pallas_call x1, Pallas kernels, body(): pl.pallas_call(kernel, out_shape=(wide, wide, jax.ShapeDtypeStruct((8, 12...  61.8 us

profile of v4, /device:TPU:1, one launch (start us, length us, event | category | flops | bytes accessed | tf_op | source)
XLA Modules:
  0.0 65.3 jit_solution(1008762611814533915)
XLA Ops:
  0.6 0.0 copy-start
  2.0 0.0 copy-done
  2.0 0.8 %concatenate.3.given_ref = f32[40,1152]{1,0:T(8,128)S(1)} concatenate(bf16[16,1152]{1,0:T(8,128)(2,1)S(1)} %copy-done, bf16[16,1152]{1,0:T(8,128)(2,1)} %param.5, f32[1,1152]{1,0:T(1,128)S(1)} %broadcast_in_dim.9, f32[1,1152]{1,0:T(1,128)S(1)} %broadcast_in_dim.10, f32[6,1152]{1,0:T(8,128)S(1)} %broadcast_in_dim.11), dimensions={0} | concatenate | bytes 294912 | tf_op jit(solution)/shard_map/concatenate | solution.py:371
  2.8 61.8 %sigmoid_loss.1 = (f32[16,1152]{1,0:T(8,128)S(1)}, f32[16,1152]{1,0:T(8,128)S(1)}, f32[8,128]{1,0:T(8,128)S(1)}) custom-call(f32[40,1152]{1,0:T(8,128)S(1)} %concatenate.3.given_ref), custom_call_target="tpu_custom_call" | custom-call | tf_op jit(solution)/shard_map/sigmoid_loss/pallas_call | solution.py:372
  64.6 0.7 %write_out.1 = (f32[1]{0:T(128)}, f32[16,1152]{1,0:T(8,128)}, f32[16,1152]{1,0:T(8,128)}, f32[1]{0:T(128)}, f32[1]{0:T(128)}) custom-call(f32[16,1152]{1,0:T(8,128)S(1)} %get-tuple-element.8.grad_images_ref, f32[16,1152]{1,0:T(8,128)S(1)} %get-tuple-element.9.grad_texts_ref, f32[8,128]{1,0:T(8,128)S(1)} %get-tuple-element.10.sums_ref), custom_call_target="tpu_custom_call" | custom-call | tf_op jit(solution)/shard_map/write_out/pallas_call | solution.py:381
  (3 shorter events, 0.0 us)
Async XLA Ops:
  0.6 1.3 %copy-start = (bf16[16,1152]{1,0:T(8,128)(2,1)S(1)}, bf16[16,1152]{1,0:T(8,128)(2,1)}, u32[]{:S(2)}) copy-start(bf16[16,1152]{1,0:T(8,128)(2,1)} %param.4) | copy-start | bytes 110596

commit v5 on v4

--- a/solution.py
+++ b/solution.py
@@ -182,14 +182,14 @@
     folded = [part[:, 0:128] + part[:, 128:256] + part[:, 256:384] + part[:, 384:512] for part in parts]
     PA[0] = jnp.concatenate(folded + [jnp.zeros((5, 128), F32)], axis=0)
 
+    text_product(6)
+    send_dy(6)
     texts_all = YB[...].reshape(512, width)
     over_texts = (((0,), (0,)), ((), ()))
     groups = ((3, 3), (1, 2), (6, 2), (0, 1))
     DXS[...] = lax.dot_general(GT[:, 256:512], texts_all, over_texts, preferred_element_type=F32).reshape(NX, 2, ROWS, width)
     for first, n in groups:
         send(f"sx{first}", DXS.at[pl.ds(first, n)], RXS.at[pl.ds(first, n)], dc=1)
-    text_product(6)
-    send_dy(6)
     for j in FAR_FIRST:
         send(f"pa{NX - j}", PA.at[0], PA.at[NX - j], dx=j)
     DX0[...] = lax.dot_general(GT[:, 0:256], texts_all, over_texts, preferred_element_type=F32).reshape(NX, 2, ROWS, width)

time: 65.7 us -> 65.7 us (level)
  no operation moved by 1% of the time
where the time goes in v5:
time: 65.7 us; the launch traced here: 65.2 us
  Pallas kernels  62.4 us (95%)
  between operations  1.98 us (3%)
  local copies, waits for them, and re-layouts  0.83 us (1%)
    pallas_call x1, Pallas kernels, body(): pl.pallas_call(kernel, out_shape=(wide, wide, jax.ShapeDtypeStruct((8, 12...  61.7 us

profile of v5, /device:TPU:1, one launch (start us, length us, event | category | flops | bytes accessed | tf_op | source)
XLA Modules:
  0.0 65.2 jit_solution(11809877110374422790)
XLA Ops:
  0.6 0.0 copy-start
  2.0 0.0 copy-done
  2.0 0.8 %concatenate.3.given_ref = f32[40,1152]{1,0:T(8,128)S(1)} concatenate(bf16[16,1152]{1,0:T(8,128)(2,1)S(1)} %copy-done, bf16[16,1152]{1,0:T(8,128)(2,1)} %param.5, f32[1,1152]{1,0:T(1,128)S(1)} %broadcast_in_dim.9, f32[1,1152]{1,0:T(1,128)S(1)} %broadcast_in_dim.10, f32[6,1152]{1,0:T(8,128)S(1)} %broadcast_in_dim.11), dimensions={0} | concatenate | bytes 294912 | tf_op jit(solution)/shard_map/concatenate | solution.py:371
  2.8 61.7 %sigmoid_loss.1 = (f32[16,1152]{1,0:T(8,128)S(1)}, f32[16,1152]{1,0:T(8,128)S(1)}, f32[8,128]{1,0:T(8,128)S(1)}) custom-call(f32[40,1152]{1,0:T(8,128)S(1)} %concatenate.3.given_ref), custom_call_target="tpu_custom_call" | custom-call | tf_op jit(solution)/shard_map/sigmoid_loss/pallas_call | solution.py:372
  64.5 0.7 %write_out.1 = (f32[1]{0:T(128)}, f32[16,1152]{1,0:T(8,128)}, f32[16,1152]{1,0:T(8,128)}, f32[1]{0:T(128)}, f32[1]{0:T(128)}) custom-call(f32[16,1152]{1,0:T(8,128)S(1)} %get-tuple-element.8.grad_images_ref, f32[16,1152]{1,0:T(8,128)S(1)} %get-tuple-element.9.grad_texts_ref, f32[8,128]{1,0:T(8,128)S(1)} %get-tuple-element.10.sums_ref), custom_call_target="tpu_custom_call" | custom-call | tf_op jit(solution)/shard_map/write_out/pallas_call | solution.py:381
  (3 shorter events, 0.0 us)
Async XLA Ops:
  0.6 1.3 %copy-start = (bf16[16,1152]{1,0:T(8,128)(2,1)S(1)}, bf16[16,1152]{1,0:T(8,128)(2,1)}, u32[]{:S(2)}) copy-start(bf16[16,1152]{1,0:T(8,128)(2,1)} %param.4) | copy-start | bytes 110596
